TPU v7x, 512 devices: a whole 4x8x8 slice. The times are simulated.
512 devices in a mesh: pool: 64 (over z, y), tensor: 8 (over x, core).
Axes of the slice: x: 4, y: 8, z: 8, core: 2. Of those that a mesh axis runs over, the one named last changes fastest.
Arguments:
- stream: bfloat16 [16, 8192], P(None, 'pool'), may hold values from -72 to 72, as said below
- norm_gain: bfloat16 [8192], P('pool'), may hold values from 0.099609375 to 1.8984375
- query_weight: bfloat16 [8192, 8192], P('pool', 'tensor'), may hold values from -0.0625 to 0.0625
- query_bias: bfloat16 [8192], P('tensor'), may hold values from -2.5 to 2.5
- key_matrix: bfloat16 [8192, 1024], P('pool', 'tensor'), may hold values from -0.0625 to 0.0625
- key_offset_bias: bfloat16 [1024], P('tensor'), may hold values from -2.5 to 2.5
- value_matrix: bfloat16 [8192, 1024], P('pool', 'tensor'), may hold values from -0.0625 to 0.0625
- value_offset_bias: bfloat16 [1024], P('tensor'), may hold values from -2.5 to 2.5
- out_weight: bfloat16 [8192, 8192], P('tensor', 'pool'), may hold values from -0.0625 to 0.0625
- key_pages: bfloat16 [1024, 128, 8, 128], P('pool', None, 'tensor'), may hold values from -52 to 52, as said below
- paged_values: bfloat16 [1024, 128, 8, 128], P('pool', None, 'tensor'), may hold values from -4 to 4
- block_table: int32 [16, 256], replicated, may hold values from -1 to 1023, as said below
- lengths: int32 [16], replicated, may hold values from 1 to 32768, as said below
Outputs:
- branch: bfloat16 [2, 16, 8192], P(None, None, 'pool')
- appended: bfloat16 [2, 2, 16, 8, 128], P(None, None, None, 'tensor')
Inputs may be any that keep to these rules, and one draw needn't show every extreme that they name: The stream rows and columns have different scales. `key_pages`: cached keys are real-valued. `lengths`: one sequence holds exactly 32768 tokens; the others hold at most 4096. block_table[s, j] names the page holding tokens j * 128 to j * 128 + 127 of sequence s for j below ceil(lengths[s] / 128), and is -1 beyond; no page is named twice; page p is held by pool index p // 16; pool indices hold unequal numbers of named pages.
All inputs are finite; a program needn't handle non-finite values.
Results may differ from a plain program's by a relative error of at most 0.03.
Values may be sent and summed in bfloat16 or wider, within the bound.
A program may use at most 64 MiB of HBM per device.

v0:
```python
import math

import jax
import jax.numpy as jnp
from jax import lax
from jax.sharding import PartitionSpec as P

MODEL_WIDTH = 8192


EPS = 1e-06
NEG = -1e30


def combined_all(value, axis, join):
    pieces = jax.tree.map(lambda part: lax.all_gather(part, axis), value)
    head = jax.tree.map(lambda part: part[0], pieces)
    tail = jax.tree.map(lambda part: part[1:], pieces)
    subtotal, _ = lax.scan(lambda subtotal, section: (join(subtotal, section), None), head, tail)
    return subtotal


def merge_terms(first, second):
    first_peak, first_total, first_mixed = first
    second_peak, second_total, second_mixed = second
    peak_max = jnp.maximum(first_peak, second_peak)
    first_factor = jnp.exp(first_peak - peak_max)
    second_factor = jnp.exp(second_peak - peak_max)
    return (
        peak_max,
        first_total * first_factor + second_total * second_factor,
        first_mixed * first_factor[..., None] + second_mixed * second_factor[..., None],
    )


def page_terms(query_pages, cached_keys, cached_values, usable, score_scale):
    scores = (
        jnp.einsum("pkgd,ptkd->pkgt", query_pages, cached_keys, preferred_element_type=jnp.float32)
        * score_scale
    )
    usable_mask = usable[:, None, None, :]
    scores = jnp.where(usable_mask, scores, NEG)
    peaks = jnp.max(scores, axis=3)
    weights = jnp.where(usable_mask, jnp.exp(scores - peaks[..., None]), 0.0).astype(jnp.bfloat16)
    totals = jnp.sum(weights.astype(jnp.float32), axis=3)
    mixed = jnp.einsum(
        "pkgt,ptkd->pkgd", weights, cached_values, preferred_element_type=jnp.float32
    )
    return (peaks, totals, mixed)


def per_sequence(peaks, totals, mixed, member):
    best = jnp.max(jnp.where(member[:, :, None, None], peaks[None], NEG), axis=1)
    scaled_weights = jnp.where(member[:, :, None, None], jnp.exp(peaks[None] - best[:, None]), 0.0)
    seq_totals = jnp.sum(scaled_weights * totals[None], axis=1)
    seq_mixed = jnp.einsum(
        "bpkg,pkgd->bkgd", scaled_weights, mixed, precision=lax.Precision.HIGHEST
    )
    return (best, seq_totals, seq_mixed)


def shards(
    stream,
    norm_gain,
    query_weight,
    query_bias,
    key_matrix,
    key_offset_bias,
    value_matrix,
    value_offset_bias,
    out_weight,
    key_pages,
    paged_values,
    block_table,
    lengths,
):
    seq_count = stream.shape[0]
    slot_count, page_len, kv_local, head_dim = key_pages.shape
    query_group = query_weight.shape[1] // (kv_local * head_dim)
    head_count = kv_local * query_group
    score_scale = 1.0 / math.sqrt(head_dim)
    first_page = lax.axis_index("pool") * slot_count
    page_ids = first_page + jnp.arange(slot_count, dtype=jnp.int32)
    matches = block_table[:, :, None] == page_ids[None, None, :]
    seq_ids = jnp.arange(seq_count, dtype=jnp.int32)
    block_ids = jnp.arange(block_table.shape[1], dtype=jnp.int32)
    member = jnp.any(matches, axis=1)
    live = jnp.any(member, axis=0)
    owner = jnp.sum(jnp.where(member, seq_ids[:, None], 0), axis=0)
    block_of = jnp.sum(jnp.where(matches, block_ids[None, :, None], 0), axis=(0, 1))
    position = block_of[:, None] * page_len + jnp.arange(page_len, dtype=jnp.int32)[None, :]
    owner_length = jnp.sum(jnp.where(member, lengths[:, None], 0), axis=0)
    usable = live[:, None] & (position < owner_length[:, None])
    current = stream
    recent = []
    branches = []
    appended = []
    for step_index in range(2):
        widened = current.astype(jnp.float32)
        scaled = (widened * norm_gain.astype(jnp.float32)).astype(jnp.bfloat16)
        partial_query = jnp.dot(scaled, query_weight, preferred_element_type=jnp.float32)
        partial_key = jnp.dot(scaled, key_matrix, preferred_element_type=jnp.float32)
        partial_value = jnp.dot(scaled, value_matrix, preferred_element_type=jnp.float32)
        squares = jnp.sum(widened * widened, axis=1)
        full_query, full_key, full_value, square_sum = lax.psum(
            (partial_query, partial_key, partial_value, squares), "pool"
        )
        inverse = lax.rsqrt(square_sum / MODEL_WIDTH + EPS)[:, None]
        query_vector = (inverse * full_query + query_bias.astype(jnp.float32)).astype(jnp.bfloat16)
        latest_key = (
            (inverse * full_key + key_offset_bias.astype(jnp.float32))
            .astype(jnp.bfloat16)
            .reshape(seq_count, kv_local, head_dim)
        )
        latest_value = (
            (inverse * full_value + value_offset_bias.astype(jnp.float32))
            .astype(jnp.bfloat16)
            .reshape(seq_count, kv_local, head_dim)
        )
        heads_of_query = query_vector.reshape(seq_count, kv_local, query_group, head_dim)
        recent.append((latest_key, latest_value))
        peaks, totals, mixed = page_terms(
            heads_of_query[owner], key_pages, paged_values, usable, score_scale
        )
        local_peak, local_total, local_mixed = per_sequence(peaks, totals, mixed, member)
        merged = combined_all((local_peak, local_total, local_mixed), "pool", merge_terms)
        for key_per_token, value_per_token in recent:
            score_per_token = (
                jnp.einsum(
                    "syou,syu->syo",
                    heads_of_query,
                    key_per_token,
                    preferred_element_type=jnp.float32,
                )
                * score_scale
            )
            mixed_per_token = jnp.broadcast_to(
                value_per_token.astype(jnp.float32)[:, :, None, :],
                (seq_count, kv_local, query_group, head_dim),
            )
            merged = merge_terms(
                merged, (score_per_token, jnp.ones_like(score_per_token), mixed_per_token)
            )
        attended = (
            (merged[2] / merged[1][..., None])
            .astype(jnp.bfloat16)
            .reshape(seq_count, head_count * head_dim)
        )
        layer_out = lax.psum(
            jnp.dot(attended, out_weight, preferred_element_type=jnp.float32), "tensor"
        )
        branches.append(layer_out.astype(jnp.bfloat16))
        appended.append(jnp.stack([latest_key, latest_value]))
        current = (current.astype(jnp.float32) + layer_out).astype(jnp.bfloat16)
    return (jnp.stack(branches), jnp.stack(appended))


def solution(mesh):
    in_specs = (
        P(None, "pool"),
        P("pool"),
        P("pool", "tensor"),
        P("tensor"),
        P("pool", "tensor"),
        P("tensor"),
        P("pool", "tensor"),
        P("tensor"),
        P("tensor", "pool"),
        P("pool", None, "tensor", None),
        P("pool", None, "tensor", None),
        P(),
        P(),
    )
    out_specs = (P(None, None, "pool"), P(None, None, None, "tensor", None))
    return jax.shard_map(shards, mesh=mesh, in_specs=in_specs, out_specs=out_specs, check_vma=False)
```

profile of v0, /device:TPU:1, one launch (start us, length us, event | category | flops | bytes accessed | tf_op | source)
XLA Modules:
  0.0 974.5 jit_solution(15935223458133817035)
XLA Ops:
  7.9 1.7 fusion.66
  10.6 0.9 fusion.20
  11.5 1.3 compare_reduce_fusion
  13.5 0.9 fusion.64
  14.4 0.9 fusion.62
  16.0 231.6 %all-reduce.1 = (f32[16]{0:T(128)S(1)}, f32[16,128]{1,0:T(8,128)S(1)}, f32[16,128]{1,0:T(8,128)S(1)}) all-reduce(f32[16]{0:T(128)S(1)} %fusion.47, f32[16,128]{1,0:T(8,128)S(1)} %fusion.64, f32[16,128]{1,0:T(8,128)S(1)} %fusion.62), channel_id=1, replica_groups=mesh['pool'=64,'tensor'=8] {'pool'}, use_global_device_ids=true, to_apply=%region_5.6 | all-reduce | flops 4112 | bytes 32896 | tf_op jit(solution)/shard_map/psum | solution.py:105
  247.7 0.9 fusion.29
  250.0 1.3 fusion.16
  251.3 0.9 convolution_bitcast_fusion.1
  254.4 34.7 %all-gather.7 = f32[64,16,8]{1,2,0:T(8,128)S(1)} all-gather(f32[1,16,8]{1,2,0:T(8,128)S(1)} %bitcast.290), channel_id=3, replica_groups=mesh['pool'=64,'tensor'=8] {'pool'}, dimensions={0}, use_global_device_ids=true | all-gather | bytes 33280 | tf_op jit(solution)/shard_map/all_gather | solution.py:16
  289.0 37.8 %all-gather.6 = f32[64,16,8]{1,2,0:T(8,128)S(1)} all-gather(f32[1,16,8]{1,2,0:T(8,128)S(1)} %bitcast.289), channel_id=2, replica_groups=mesh['pool'=64,'tensor'=8] {'pool'}, dimensions={0}, use_global_device_ids=true | all-gather | bytes 33280 | tf_op jit(solution)/shard_map/all_gather | solution.py:16
  326.9 58.7 %all-gather.13.cloned.1.call-done = f32[1024,1,8,128]{3,0,2,1:T(8,128)} async-done(((f32[16,1,8,128]{3,0,2,1:T(8,128)}), f32[1024,1,8,128]{3,0,2,1:T(8,128)}) %all-gather.13.cloned.1.call-update) | async-done | bytes 4194320 | tf_op jit(solution)/shard_map/all_gather | solution.py:16
  386.5 4.4 slice.77
  391.0 73.3 %while.28 = (s32[]{:T(128)}, f32[16,1,8]{0,2,1:T(8,128)S(1)}, f32[16,1,8]{0,2,1:T(8,128)S(1)}, f32[16,1,8,128]{3,2,1,0:T(8,128)S(1)}, f32[63,16,1,8]{1,3,2,0:T(8...) while((s32[]{:T(128)}, f32[16,1,8]{0,2,1:T(8,128)S(1)}, ...), condition=%wide.region_13.14_spmd, body=%wide.region_12.13_spmd.sunk | while | flops 50050 | bytes 337513 | solution.py:19
  391.2 0.8 constant_dynamic-slice_fusion.4
  392.3 0.8 constant_dynamic-slice_fusion.4
  393.5 0.8 constant_dynamic-slice_fusion.4
  394.7 0.8 constant_dynamic-slice_fusion.4
  395.8 0.8 constant_dynamic-slice_fusion.4
  397.0 0.8 constant_dynamic-slice_fusion.4
  398.2 0.8 constant_dynamic-slice_fusion.4
  399.3 0.8 constant_dynamic-slice_fusion.4
  400.5 0.8 constant_dynamic-slice_fusion.4
  401.6 0.8 constant_dynamic-slice_fusion.4
  402.8 0.8 constant_dynamic-slice_fusion.4
  404.0 0.8 constant_dynamic-slice_fusion.4
  405.1 0.8 constant_dynamic-slice_fusion.4
  406.3 0.8 constant_dynamic-slice_fusion.4
  407.5 0.8 constant_dynamic-slice_fusion.4
  408.6 0.8 constant_dynamic-slice_fusion.4
  409.8 0.8 constant_dynamic-slice_fusion.4
  410.9 0.8 constant_dynamic-slice_fusion.4
  412.1 0.8 constant_dynamic-slice_fusion.4
  413.3 0.8 constant_dynamic-slice_fusion.4
  414.4 0.8 constant_dynamic-slice_fusion.4
  415.6 0.8 constant_dynamic-slice_fusion.4
  416.8 0.8 constant_dynamic-slice_fusion.4
  417.9 0.8 constant_dynamic-slice_fusion.4
  419.1 0.8 constant_dynamic-slice_fusion.4
  429.6 0.8 constant_dynamic-slice_fusion.4
  430.7 0.8 constant_dynamic-slice_fusion.4
  441.2 0.8 constant_dynamic-slice_fusion.4
  451.7 0.8 constant_dynamic-slice_fusion.4
  452.8 0.8 constant_dynamic-slice_fusion.4
  463.3 0.8 constant_dynamic-slice_fusion.4
  464.8 32.0 %psum.74 = f32[16,128]{1,0:T(8,128)S(1)} all-reduce(f32[16,128]{1,0:T(8,128)S(1)} %fusion.34), channel_id=1, replica_groups=mesh['pool'=64,'tensor'=8] {'tensor'}, use_global_device_ids=true, to_apply=%region_16.17 | all-reduce | flops 2048 | bytes 16384 | tf_op jit(solution)/shard_map/psum | solution.py:149
  498.0 221.5 %all-reduce = (f32[16]{0:T(128)S(1)}, f32[16,128]{1,0:T(8,128)S(1)}, f32[16,128]{1,0:T(8,128)S(1)}) all-reduce(f32[16]{0:T(128)S(1)} %get-tuple-element.192, f32[16,128]{1,0:T(8,128)S(1)} %fusion.70, f32[16,128]{1,0:T(8,128)S(1)} %fusion.68), channel_id=1, replica_groups=mesh['pool'=64,'tensor'=8] {'pool'}, use_global_device_ids=true, to_apply=%region_18.19 | all-reduce | flops 4112 | bytes 32896 | tf_op jit(solution)/shard_map/psum | solution.py:105
  719.5 0.9 fusion.30
  722.0 0.9 convolution_bitcast_fusion
  724.6 34.7 %all-gather.9 = f32[64,16,8]{1,2,0:T(8,128)S(1)} all-gather(f32[1,16,8]{1,2,0:T(8,128)S(1)} %bitcast.291), channel_id=6, replica_groups=mesh['pool'=64,'tensor'=8] {'pool'}, dimensions={0}, use_global_device_ids=true | all-gather | bytes 33280 | tf_op jit(solution)/shard_map/all_gather | solution.py:16
  759.3 36.7 %all-gather.8 = f32[64,16,8]{1,2,0:T(8,128)S(1)} all-gather(f32[1,16,8]{1,2,0:T(8,128)S(1)} %bitcast.288), channel_id=5, replica_groups=mesh['pool'=64,'tensor'=8] {'pool'}, dimensions={0}, use_global_device_ids=true | all-gather | bytes 33280 | tf_op jit(solution)/shard_map/all_gather | solution.py:16
  796.1 59.7 %all-gather.15.cloned.1.call-done = f32[1024,1,8,128]{3,0,2,1:T(8,128)} async-done(((f32[16,1,8,128]{3,0,2,1:T(8,128)}), f32[1024,1,8,128]{3,0,2,1:T(8,128)}) %all-gather.15.cloned.1.call-update) | async-done | bytes 4194320 | tf_op jit(solution)/shard_map/all_gather | solution.py:16
  856.7 4.4 slice.83
  861.0 73.3 %while.29 = (s32[]{:T(128)}, f32[16,1,8]{0,2,1:T(8,128)S(1)}, f32[16,1,8]{0,2,1:T(8,128)S(1)}, f32[16,1,8,128]{3,2,1,0:T(8,128)S(1)}, f32[63,16,1,8]{1,3,2,0:T(8...) while((s32[]{:T(128)}, f32[16,1,8]{0,2,1:T(8,128)S(1)}, ...), condition=%wide.region_25.26_spmd, body=%wide.region_24.25_spmd.sunk | while | flops 50050 | bytes 337513 | solution.py:19
  870.5 0.8 constant_dynamic-slice_fusion.5
  881.0 0.8 constant_dynamic-slice_fusion.5
  882.2 0.8 constant_dynamic-slice_fusion.5
  892.6 0.8 constant_dynamic-slice_fusion.5
  903.1 0.8 constant_dynamic-slice_fusion.5
  904.3 0.8 constant_dynamic-slice_fusion.5
  914.7 0.8 constant_dynamic-slice_fusion.5
  925.2 0.8 constant_dynamic-slice_fusion.5
  926.4 0.8 constant_dynamic-slice_fusion.5
  935.0 32.3 %psum.79 = bf16[16,128]{1,0:T(8,128)(2,1)S(1)} all-reduce(f32[16,128]{1,0:T(8,128)S(1)} %fusion.31), channel_id=1, replica_groups=mesh['pool'=64,'tensor'=8] {'tensor'}, use_global_device_ids=true, to_apply=%region_28.29 | all-reduce | flops 2048 | bytes 12288 | tf_op jit(solution)/shard_map/psum | solution.py:149
  (942 shorter events, 122.7 us)
Async XLA Ops:
  7.2 242.1 %copy-start = (bf16[16,128,1,128]{3,1,2,0:T(8,128)(2,1)S(1)}, bf16[16,128,1,128]{3,1,2,0:T(8,128)(2,1)}, u32[]{:S(2)}) copy-start(bf16[16,128,1,128]{3,1,2,0:T(8,128)(2,1)} %param.26) | copy-start | bytes 1572868
  7.2 240.5 %all-reduce.5.cloned.1.call-start = ((), (), s32[]{:S(2)}) async-start(), calls=%async_computation | async-start | bytes 131072 | tf_op jit(solution)/shard_map/psum | solution.py:105
  9.7 375.9 %all-gather.13.cloned.1.call-start = ((), (), s32[]{:S(2)}) async-start(), calls=%async_computation.2 | async-start | bytes 4259840 | tf_op jit(solution)/shard_map/all_gather | solution.py:16
  252.2 467.3 %all-reduce.7.cloned.1.call-start = ((), (), s32[]{:S(2)}) async-start(), calls=%async_computation.1 | async-start | bytes 131072 | tf_op jit(solution)/shard_map/psum | solution.py:105
  386.5 78.1 %copy-start.2 = (bf16[1024,128]{1,0:T(8,128)(2,1)S(1)}, bf16[1024,128]{1,0:T(8,128)(2,1)}, u32[]{:S(2)}) copy-start(bf16[1024,128]{1,0:T(8,128)(2,1)} %param.25) | copy-start | bytes 786436
  386.5 110.3 %copy-start.6 = (bf16[16,128]{1,0:T(8,128)(2,1)S(1)}, bf16[16,128]{1,0:T(8,128)(2,1)}, u32[]{:S(2)}) copy-start(bf16[16,128]{1,0:T(8,128)(2,1)} %param.17) | copy-start | bytes 12292
  386.5 110.4 %copy-start.4 = (bf16[128,128]{1,0:T(8,128)(2,1)S(1)}, bf16[128,128]{1,0:T(8,128)(2,1)}, u32[]{:S(2)}) copy-start(bf16[128,128]{1,0:T(8,128)(2,1)} %param.23) | copy-start | bytes 98308
  386.5 110.5 %copy-start.5 = (bf16[128,128]{1,0:T(8,128)(2,1)S(1)}, bf16[128,128]{1,0:T(8,128)(2,1)}, u32[]{:S(2)}) copy-start(bf16[128,128]{1,0:T(8,128)(2,1)} %param.21) | copy-start | bytes 98308
  386.5 110.6 %copy-start.3 = (bf16[128,1024]{1,0:T(8,128)(2,1)S(1)}, bf16[128,1024]{1,0:T(8,128)(2,1)}, u32[]{:S(2)}) copy-start(bf16[128,1024]{1,0:T(8,128)(2,1)} %param.19) | copy-start | bytes 786436
  391.0 330.7 %copy-start.1 = (bf16[16,128,1,128]{3,1,2,0:T(8,128)(2,1)S(1)}, bf16[16,128,1,128]{3,1,2,0:T(8,128)(2,1)}, u32[]{:S(2)}) copy-start(bf16[16,128,1,128]{3,1,2,0:T(8,128)(2,1)} %param.27) | copy-start | bytes 1572868
  498.0 357.8 %all-gather.15.cloned.1.call-start = ((), (), s32[]{:S(2)}) async-start(), calls=%async_computation.3 | async-start | bytes 4259840 | tf_op jit(solution)/shard_map/all_gather | solution.py:16
Sparse Core Ops, SparseCore 0:
  11.2 150.0 all-reduce.4
  252.3 133.2 all-gather.12
  498.1 135.7 all-reduce.6
  723.1 132.6 all-gather.14
where the time goes:
time: 981 us; the launch traced here: 974 us
  blocking collectives  661 us (67%)
  local copies, waits for them, and re-layouts  138 us (14%)
  waiting for transfers between devices  118 us (12%)
  other arithmetic  28 us (3%)
  between operations  14.1 us (1%)
    psum x2, blocking collectives, shards(): lax.psum((partial_query, partial_key, partial_value, squares), 'pool')  453 us
    all_gather x4, blocking collectives, combined_all(): pieces = jax.tree.map(lambda part: lax.all_gather(part, axis), value)  144 us
    all_gather x2, waiting for transfers between devices, combined_all(): pieces = jax.tree.map(lambda part: lax.all_gather(part, axis), value)  118 us
    dynamic_slice x126, local copies, waits for them, and re-layouts, combined_all(): lax.scan(lambda subtotal, section: (join(subtotal, section), None), head,...  107 us
    psum x2, blocking collectives, shards(): lax.psum(jnp.dot(attended, out_weight, preferred_element_type=jnp.float32...  64.3 us
  transfers between devices with their start and end apart: 4, of which 2 were waited for; matrix products, arithmetic and copies ran while one was open for 1% of the time, Pallas kernels for 0%

commit v1 on v0

v1 whole, which is shorter than its diff:
```python
import functools
import math

import jax
import jax.numpy as jnp
from jax import lax
from jax.experimental import pallas as pl
from jax.experimental.pallas import tpu as pltpu
from jax.sharding import PartitionSpec as P

MESH = pl.DeviceIdType.MESH
EPS = 1e-06
NEG = -1e30
STEPS = 2
SEQS = 16
GROUP = 8
HEAD = 128
HALF = 64
RING = 8
PAGE = 128
SLOTS = 16
LANES = GROUP * SEQS
FAR_FIRST = (4, 3, 5, 2, 6, 1, 7)
BF16 = jnp.bfloat16
F32 = jnp.float32

A1_Y, A1_Z, A1_SQ, A2_Z, A2_Y, A2_SQ, K1, V1, K2, V2 = range(10)
B1_Y, B1_Z, B1_SY, B1_SZ, B2_Z, B2_Y, B2_SZ, B2_SY, C_T = range(10, 19)
EXCHANGES = 19


def dot(a, b):
    return jnp.dot(a, b, preferred_element_type=F32)


def kernel(
    width,
    x_hbm, gain_hbm, wq_hbm, bq_hbm, wk_hbm, bk_hbm, wv_hbm, bv_hbm, wo_hbm, keys_hbm, values_hbm, table_hbm, lengths_ref,
    branch_ref, appended_ref,
    x_ref, gain_ref, wq, bq, wk, bk, wv, bv, wo, keys, values, table,
    values_t, limits, bias_t,
    big, stat, small,
    local_sem, send_sem, recv_sem,
):
    pool, tensor = lax.axis_index("pool"), lax.axis_index("tensor")
    z, y = pool // RING, lax.rem(pool, RING)

    def on_ring(axis, distance):
        if axis == "y":
            return (z * RING + lax.rem(y + distance, RING), tensor)
        if axis == "z":
            return (lax.rem(z + distance, RING) * RING + y, tensor)
        return (pool, lax.rem(tensor + distance, RING))

    place = {"y": y, "z": z, "t": tensor}
    axis_of = {
        A1_Y: "y", A1_Z: "z", A1_SQ: "y", A2_Z: "z", A2_Y: "y", A2_SQ: "z", K1: "y", V1: "z", K2: "z", V2: "y",
        B1_Y: "y", B1_Z: "z", B1_SY: "y", B1_SZ: "z", B2_Z: "z", B2_Y: "y", B2_SZ: "z", B2_SY: "y", C_T: "t",
    }
    big_at = {name: at for at, name in enumerate((A1_Y, A1_Z, A2_Z, A2_Y, B1_Y, B1_Z, B2_Z, B2_Y))}
    stat_at = {name: at for at, name in enumerate((A1_SQ, A2_SQ, B1_SY, B1_SZ, B2_SZ, B2_SY))}
    small_at = {name: at for at, name in enumerate((K1, V1, K2, V2, C_T))}

    def slots(step, name):
        for ref, at in ((big, big_at), (stat, stat_at), (small, small_at)):
            if name in at:
                return ref.at[step, at[name]]

    def fill(step, name, value):
        ref = slots(step, name)
        ref[place[axis_of[name]]] = value.astype(ref.dtype)

    def send(step, *names):
        for distance in FAR_FIRST:
            for name in names:
                own = slots(step, name).at[place[axis_of[name]]]
                pltpu.make_async_remote_copy(
                    src_ref=own, dst_ref=own,
                    send_sem=send_sem.at[step, name], recv_sem=recv_sem.at[step, name],
                    device_id=on_ring(axis_of[name], distance), device_id_type=MESH,
                ).start()

    def others(step, name, sem):
        part = slots(step, name).at[pl.ds(0, RING - 1)]
        pltpu.make_async_copy(part, part, sem.at[step, name]).wait()

    def receive(step, *names):
        for name in names:
            others(step, name, recv_sem)
        return [slots(step, name)[...].astype(F32) for name in names]

    barrier = pltpu.get_barrier_semaphore()
    for axis in ("y", "z", "t"):
        for distance in FAR_FIRST:
            pl.semaphore_signal(barrier, inc=1, device_id=on_ring(axis, distance), device_id_type=MESH)

    pairs = (
        (x_hbm, x_ref), (gain_hbm, gain_ref), (wq_hbm, wq), (wk_hbm, wk), (wv_hbm, wv), (bq_hbm, bq), (bk_hbm, bk),
        (bv_hbm, bv), (table_hbm, table), (values_hbm, values), (keys_hbm, keys), (wo_hbm, wo),
    )
    loads = [pltpu.make_async_copy(src, dst, local_sem.at[at]) for at, (src, dst) in enumerate(pairs)]
    for load in loads:
        load.start()
    for load in loads[:3]:
        load.wait()

    lane = lax.broadcasted_iota(jnp.int32, (1, LANES), 1)
    lane_seq = lax.rem(lane, SEQS)
    own_seq = lax.broadcasted_iota(jnp.int32, (SEQS, LANES), 0) == lane_seq
    scale = 1.0 / math.sqrt(HEAD)

    def tiled(rows):
        return jnp.concatenate([rows] * GROUP, axis=0)

    def project(current):
        scaled = (current * gain_ref[...].astype(F32)).astype(BF16)
        raw = dot(scaled, wq[...])
        raw = jnp.concatenate([raw[:, h * HEAD:(h + 1) * HEAD] for h in range(GROUP)], axis=0)
        squares = jnp.sum(tiled(current * current).T, axis=0, keepdims=True)
        return scaled, raw.T, squares

    def merged(peaks, outs):
        top = peaks[0]
        for i in range(1, len(peaks)):
            top = jnp.maximum(top, peaks[i])
        weights = [jnp.exp(peak - top) for peak in peaks]
        total, out = weights[0], weights[0] * outs[0]
        for weight, part in zip(weights[1:], outs[1:]):
            total = total + weight
            out = out + weight * part
        return top + jnp.log(total), out / total

    current = x_ref[...].astype(F32)
    recent = []
    for step in range(STEPS):
        scaled, raw_t, squares = project(current)
        fill(step, A1_Y, raw_t[:HALF])
        fill(step, A1_Z, raw_t[HALF:])
        fill(step, A1_SQ, squares)
        if step == 0:
            pl.semaphore_wait(barrier, 3 * (RING - 1))
        send(step, A1_Y, A1_Z, A1_SQ)
        if step == 0:
            for load in loads[3:5]:
                load.wait()
        fill(step, K1, dot(scaled, wk[...]))
        fill(step, V1, dot(scaled, wv[...]))
        send(step, K1, V1)

        if step == 0:
            for load in loads[5:10]:
                load.wait()
            bias = jnp.concatenate(
                [jnp.broadcast_to(bq[h:h + 1, :].astype(F32), (SEQS, HEAD)) for h in range(GROUP)], axis=0
            )
            bias_t[...] = bias.T
            length_row = jnp.zeros((1, LANES), jnp.int32)
            for s in range(SEQS):
                length_row = jnp.where(lane_seq == s, lengths_ref[s], length_row)
            table_t = tiled(table[...].astype(F32)).T
            blocks = table_t.shape[0]
            left = length_row.astype(F32) - PAGE * lax.broadcasted_iota(jnp.int32, (blocks, LANES), 0).astype(F32)
            first_page = pool * SLOTS
            for slot in range(SLOTS):
                wanted = (first_page + slot).astype(F32)
                limits[slot:slot + 1, :] = jnp.max(jnp.where(table_t == wanted, left, 0.0), axis=0, keepdims=True)
            for slot in range(SLOTS):
                span = pl.ds(slot * PAGE, PAGE)
                values_t[:, span] = values[span, :].T

        y_parts, z_parts, square_parts = receive(step, A1_Y, A1_Z, A1_SQ)
        fill(step, A2_Z, jnp.sum(y_parts, axis=0))
        fill(step, A2_Y, jnp.sum(z_parts, axis=0))
        fill(step, A2_SQ, jnp.sum(square_parts, axis=0))
        send(step, A2_Z, A2_Y, A2_SQ)
        k_parts, v_parts = receive(step, K1, V1)
        fill(step, K2, jnp.sum(k_parts, axis=0))
        fill(step, V2, jnp.sum(v_parts, axis=0))
        send(step, K2, V2)
        z_parts, y_parts, square_parts = receive(step, A2_Z, A2_Y, A2_SQ)
        inverse = lax.rsqrt(jnp.sum(square_parts, axis=0) / width + EPS)
        raw_t = jnp.concatenate([jnp.sum(z_parts, axis=0), jnp.sum(y_parts, axis=0)], axis=0)
        query_t = (inverse * raw_t + bias_t[...]).astype(BF16)

        if step == 0:
            loads[10].wait()
        scores = (dot(keys[...], query_t) * scale).reshape(SLOTS, PAGE, LANES)
        usable = lax.broadcasted_iota(jnp.int32, scores.shape, 1).astype(F32) < limits[...][:, None, :]
        scores = jnp.where(usable, scores, NEG)
        peak = jnp.max(jnp.max(scores, axis=0), axis=0, keepdims=True)
        weights = jnp.where(usable, jnp.exp(scores - peak[None]), 0.0).astype(BF16)
        total = jnp.sum(jnp.sum(weights.astype(F32), axis=0), axis=0, keepdims=True)
        out_t = dot(values_t[...], weights.reshape(SLOTS * PAGE, LANES))
        some = total > 0.0
        safe = jnp.where(some, total, 1.0)
        log_total = jnp.where(some, peak + jnp.log(safe), NEG)
        out_t = out_t / safe
        fill(step, B1_Y, out_t[:HALF])
        fill(step, B1_Z, out_t[HALF:])
        fill(step, B1_SY, log_total)
        fill(step, B1_SZ, log_total)
        send(step, B1_Y, B1_Z, B1_SY, B1_SZ)

        k_parts, v_parts = receive(step, K2, V2)
        inverse_rows = jnp.broadcast_to(inverse, (LANES, LANES)).T[:SEQS]
        latest_key = (inverse_rows * jnp.sum(k_parts, axis=0) + bk[...].astype(F32)).astype(BF16)
        latest_value = (inverse_rows * jnp.sum(v_parts, axis=0) + bv[...].astype(F32)).astype(BF16)
        appended_ref[step, 0] = latest_key
        appended_ref[step, 1] = latest_value
        recent.append((latest_key, tiled(latest_value.astype(F32)).T))
        new_scores = [
            jnp.sum(jnp.where(own_seq, dot(key, query_t), 0.0), axis=0, keepdims=True) * scale for key, _ in recent
        ]
        new_total, new_out = merged(new_scores, [value for _, value in recent])

        def gather(first, second, first_stat, second_stat):
            one, two, one_stat, two_stat = receive(step, first, second, first_stat, second_stat)
            return (
                [one_stat[i] for i in range(RING)], [one[i] for i in range(RING)],
                [two_stat[i] for i in range(RING)], [two[i] for i in range(RING)],
            )

        one_stat, one, two_stat, two = gather(B1_Y, B1_Z, B1_SY, B1_SZ)
        one_stat, one = merged(one_stat, one)
        two_stat, two = merged(two_stat, two)
        fill(step, B2_Z, one)
        fill(step, B2_Y, two)
        fill(step, B2_SZ, one_stat)
        fill(step, B2_SY, two_stat)
        send(step, B2_Z, B2_Y, B2_SZ, B2_SY)
        one_stat, one, two_stat, two = gather(B2_Z, B2_Y, B2_SZ, B2_SY)
        _, one = merged(one_stat + [new_total], one + [new_out[:HALF]])
        _, two = merged(two_stat + [new_total], two + [new_out[HALF:]])
        attended = jnp.concatenate([one, two], axis=0).T.astype(BF16)
        attended = jnp.concatenate([attended[h * SEQS:(h + 1) * SEQS] for h in range(GROUP)], axis=1)
        if step == 0:
            loads[11].wait()
        fill(step, C_T, dot(attended, wo[...]))
        send(step, C_T)
        (layer_parts,) = receive(step, C_T)
        layer = layer_parts[0]
        for i in range(1, RING):
            layer = layer + layer_parts[i]
        branch_ref[step] = layer.astype(BF16)
        current = (current + layer).astype(BF16).astype(F32)

    for step in range(STEPS):
        for name in range(EXCHANGES):
            others(step, name, send_sem)


def shards(
    stream, norm_gain, query_weight, query_bias, key_matrix, key_offset_bias, value_matrix, value_offset_bias,
    out_weight, key_pages, paged_values, block_table, lengths, *, width,
):
    tokens = SLOTS * PAGE
    operands = (
        stream, norm_gain.reshape(1, HEAD), query_weight, query_bias.reshape(GROUP, HEAD),
        key_matrix, key_offset_bias.reshape(1, HEAD), value_matrix, value_offset_bias.reshape(1, HEAD),
        out_weight, key_pages.reshape(tokens, HEAD), paged_values.reshape(tokens, HEAD), block_table, lengths,
    )
    anywhere = pl.BlockSpec(memory_space=pl.ANY)
    branch, appended = pl.pallas_call(
        functools.partial(kernel, width),
        out_shape=(
            jax.ShapeDtypeStruct((STEPS, SEQS, HEAD), BF16),
            jax.ShapeDtypeStruct((STEPS, 2, SEQS, HEAD), BF16),
        ),
        in_specs=[anywhere] * 12 + [pl.BlockSpec(memory_space=pltpu.SMEM)],
        out_specs=(pl.BlockSpec(memory_space=pltpu.VMEM), pl.BlockSpec(memory_space=pltpu.VMEM)),
        scratch_shapes=[pltpu.VMEM(operand.shape, operand.dtype) for operand in operands[:12]] + [
            pltpu.VMEM((HEAD, tokens), BF16),
            pltpu.VMEM((SLOTS, LANES), F32),
            pltpu.VMEM((HEAD, LANES), F32),
            pltpu.VMEM((STEPS, 8, RING, HALF, LANES), BF16),
            pltpu.VMEM((STEPS, 6, RING, 1, LANES), F32),
            pltpu.VMEM((STEPS, 5, RING, SEQS, HEAD), BF16),
            pltpu.SemaphoreType.DMA((12,)),
            pltpu.SemaphoreType.DMA((STEPS, EXCHANGES)),
            pltpu.SemaphoreType.DMA((STEPS, EXCHANGES)),
        ],
        compiler_params=pltpu.CompilerParams(
            collective_id=0, has_side_effects=True, vmem_limit_bytes=48 * 2**20
        ),
        cost_estimate=pl.CostEstimate(flops=400_000_000, bytes_accessed=2_000_000, transcendentals=600_000),
    )(*operands)
    return branch, appended.reshape(STEPS, 2, SEQS, 1, HEAD)


def solution(mesh):
    in_specs = (
        P(None, "pool"), P("pool"), P("pool", "tensor"), P("tensor"), P("pool", "tensor"), P("tensor"),
        P("pool", "tensor"), P("tensor"), P("tensor", "pool"), P("pool", None, "tensor", None),
        P("pool", None, "tensor", None), P(), P(),
    )
    out_specs = (P(None, None, "pool"), P(None, None, None, "tensor", None))
    width = mesh.shape["pool"] * HEAD
    return jax.shard_map(
        functools.partial(shards, width=width), mesh=mesh, in_specs=in_specs, out_specs=out_specs, check_vma=False
    )
```

time: 981 us -> 79 us (0.08)
  blocking collectives: 661 us -> 0 us
  local copies, waits for them, and re-layouts: 138 us -> 8.1 us
  waiting for transfers between devices: 118 us -> 0 us
  Pallas kernels: 0 us -> 69.7 us
  other arithmetic: 28 us -> 0 us
  between operations: 14.1 us -> 0.7 us
    psum x4 -> x0, blocking collectives: 517 us -> none  [the longest x2 453 us: shards(): lax.psum((partial_query, partial_key, partial_value, squares), 'pool')]
    all_gather x4 -> x0, blocking collectives: 144 us -> none  [combined_all(): pieces = jax.tree.map(lambda part: lax.all_gather(part, axis), value)]
    all_gather x2 -> x0, waiting for transfers between devices: 118 us -> none  [combined_all(): pieces = jax.tree.map(lambda part: lax.all_gather(part, axis), value)]
    dynamic_slice x126 -> x0, local copies, waits for them, and re-layouts: 107 us -> none  [combined_all(): lax.scan(lambda subtotal, section: (join(subtotal, section), None), head,...]
    pallas_call x0 -> x1, Pallas kernels: none -> 69.7 us  [shards(): pl.pallas_call(functools.partial(kernel, width), out_shape=(jax.ShapeDtyp...]
    mul x258 -> x0, local copies, waits for them, and re-layouts: 18.6 us -> none  [the longest x129 9.3 us: merge_terms(): first_mixed * first_factor[..., None]]
    add x127 -> x0, other arithmetic: 13.9 us -> none  [the longest x126 13.9 us: merge_terms(): first_mixed * first_factor[..., None]]
    slice x4 -> x0, local copies, waits for them, and re-layouts: 10.5 us -> none  [the longest x2 8.84 us: combined_all(): tail = jax.tree.map(lambda part: part[1:], pieces)]
  transfers between devices with their start and end apart: 4 -> 0, of which waited for: 2 -> 0; matrix products, arithmetic and copies ran while one was open for 1% -> 0% of each run, Pallas kernels for 0% -> 0%
where the time goes in v1:
time: 79 us; the launch traced here: 78.5 us
  Pallas kernels  69.7 us (88%)
  local copies, waits for them, and re-layouts  8.1 us (10%)
    pallas_call x1, Pallas kernels, shards(): pl.pallas_call(functools.partial(kernel, width), out_shape=(jax.ShapeDtyp...  69.7 us
    unnamed x28, local copies, waits for them, and re-layouts  8.1 us

profile of v1, /device:TPU:1, one launch (start us, length us, event | category | flops | bytes accessed | tf_op | source)
XLA Modules:
  0.0 78.5 jit_solution(7773336596612998393)
XLA Ops:
  0.6 0.0 copy-start.12
  0.6 0.0 copy-start.7
  0.7 0.0 copy-start.8
  0.7 0.0 copy-start.9
  0.7 0.0 copy-start.10
  0.7 0.0 copy-start.11
  0.7 0.6 copy-done.12
  1.3 0.0 copy-done.7
  1.3 0.0 copy-done.8
  1.3 0.0 copy-done.9
  1.4 0.0 copy-done.10
  1.4 0.0 copy-done.11
  1.4 0.0 copy-start
  1.4 1.0 %copy-done = bf16[16,128,1,128]{3,1,2,0:T(8,128)(2,1)S(1)} copy-done((bf16[16,128,1,128]{3,1,2,0:T(8,128)(2,1)S(1)}, bf16[16,128,1,128]{3,1,2,0:T(8,128)(2,1)}, u32[]{:S(2)}) %copy-start) | copy-done | bytes 524312
  2.4 0.0 copy-start.1
  2.4 1.0 %copy-done.1 = bf16[16,128,1,128]{3,1,2,0:T(8,128)(2,1)S(1)} copy-done((bf16[16,128,1,128]{3,1,2,0:T(8,128)(2,1)S(1)}, bf16[16,128,1,128]{3,1,2,0:T(8,128)(2,1)}, u32[]{:S(2)}) %copy-start.1) | copy-done | bytes 524312
  3.5 0.0 copy-start.2
  3.5 0.9 %copy-done.2 = bf16[128,1024]{1,0:T(8,128)(2,1)S(1)} copy-done((bf16[128,1024]{1,0:T(8,128)(2,1)S(1)}, bf16[128,1024]{1,0:T(8,128)(2,1)}, u32[]{:S(2)}) %copy-start.2) | copy-done | bytes 262168
  4.4 0.0 copy-start.3
  4.4 0.9 %copy-done.3 = bf16[1024,128]{1,0:T(8,128)(2,1)S(1)} copy-done((bf16[1024,128]{1,0:T(8,128)(2,1)S(1)}, bf16[1024,128]{1,0:T(8,128)(2,1)}, u32[]{:S(2)}) %copy-start.3) | copy-done | bytes 262168
  5.4 0.0 copy-start.4
  5.4 0.8 copy-done.4
  6.1 0.0 copy-start.5
  6.1 0.8 copy-done.5
  6.9 0.0 copy-start.6
  6.9 0.7 copy-done.6
  7.6 69.7 %shard_map.140 = (bf16[2,16,128]{2,1,0:T(8,128)(2,1)S(1)}, bf16[2,2,16,128]{3,2,1,0:T(8,128)(2,1)S(1)}) custom-call(bf16[16,128]{1,0:T(8,128)(2,1)S(1)} %copy-done.7, bf16[1,128]{1,0:T(2,128)(2,1)S(1)} %bitcast.13, bf16[128,1024]{1,0:T(8,128)(2,1)S(1)} %copy-done.2, bf16[8,128]{1,0:T(8,128)(2,1)S(1)} %bitcast.12, bf16[128,128]{1,0:T(8,128)(2,1)S(1)} %copy-done.4, ...), custom_call_target="tpu_custom_call" | custom-call | flops 400000000 | bytes 2000000 | tf_op jit(solution)/shard_map/pallas_call | solution.py:263
  77.3 0.6 copy.18
  77.9 0.6 copy.19
Async XLA Ops:
  0.6 0.7 copy-start.12
  0.6 0.7 copy-start.7
  0.7 0.7 copy-start.8
  0.7 0.7 copy-start.9
  0.7 0.7 copy-start.10
  0.7 0.7 copy-start.11
  1.4 1.0 %copy-start = (bf16[16,128,1,128]{3,1,2,0:T(8,128)(2,1)S(1)}, bf16[16,128,1,128]{3,1,2,0:T(8,128)(2,1)}, u32[]{:S(2)}) copy-start(bf16[16,128,1,128]{3,1,2,0:T(8,128)(2,1)} %param.22) | copy-start | bytes 1572868
  2.4 1.0 %copy-start.1 = (bf16[16,128,1,128]{3,1,2,0:T(8,128)(2,1)S(1)}, bf16[16,128,1,128]{3,1,2,0:T(8,128)(2,1)}, u32[]{:S(2)}) copy-start(bf16[16,128,1,128]{3,1,2,0:T(8,128)(2,1)} %param.23) | copy-start | bytes 1572868
  3.5 0.9 %copy-start.2 = (bf16[128,1024]{1,0:T(8,128)(2,1)S(1)}, bf16[128,1024]{1,0:T(8,128)(2,1)}, u32[]{:S(2)}) copy-start(bf16[128,1024]{1,0:T(8,128)(2,1)} %wq_hbm.1) | copy-start | bytes 786436
  4.4 0.9 %copy-start.3 = (bf16[1024,128]{1,0:T(8,128)(2,1)S(1)}, bf16[1024,128]{1,0:T(8,128)(2,1)}, u32[]{:S(2)}) copy-start(bf16[1024,128]{1,0:T(8,128)(2,1)} %wo_hbm.1) | copy-start | bytes 786436
  5.4 0.8 copy-start.4
  6.1 0.8 copy-start.5
  6.9 0.7 copy-start.6

commit v2 on v1

v2 whole, which is shorter than its diff:
```python
import functools
import math

import jax
import jax.numpy as jnp
from jax import lax
from jax.experimental import pallas as pl
from jax.experimental.pallas import tpu as pltpu
from jax.sharding import PartitionSpec as P

MESH = pl.DeviceIdType.MESH
EPS = 1e-06
NEG = -1e30
STEPS = 2
SEQS = 16
GROUP = 8
HEAD = 128
RING = 8
PAGE = 128
SLOTS = 16
LANES = GROUP * SEQS
TOKENS = SLOTS * PAGE
ONES = 16
CHUNK = 256
LOG2E = math.log2(math.e)
FAR_FIRST = (4, 3, 5, 2, 6, 1, 7)
BF16 = jnp.bfloat16
F32 = jnp.float32

PAIRS = 2
ROWS = HEAD // (2 * PAIRS)
RINGS = "yz"
PHASES = ("A1", "A2", "B1", "B2")


def all_streams():
    streams = {}
    for phase in PHASES:
        for chain in range(2 * PAIRS):
            streams[phase, chain] = ("rows", RINGS[(chain + PHASES.index(phase)) % 2])
    for phase, name, ring in (("A1", "k", "y"), ("A1", "v", "z"), ("A2", "k", "z"), ("A2", "v", "y"), ("C", "layer", "t")):
        streams[phase, name] = ("small", ring)
    for phase, name, ring in (
        ("A1", "squares", "y"), ("A2", "squares", "z"),
        ("B1", "first", "y"), ("B1", "second", "z"), ("B2", "first", "z"), ("B2", "second", "y"),
    ):
        streams[phase, name] = ("stat", ring)
    kinds = {"rows": 0, "small": 0, "stat": 0}
    placed = {}
    for at, (key, (kind, ring)) in enumerate(streams.items()):
        placed[key] = (kind, kinds[kind], ring, at)
        kinds[kind] += 1
    return placed, kinds


STREAMS, COUNTS = all_streams()


def dot(a, b):
    return jnp.dot(a, b, preferred_element_type=F32)


def dot_rows(a, b):
    return lax.dot_general(a, b, (((1,), (1,)), ((), ())), preferred_element_type=F32)


def kernel(
    width,
    x_hbm, gain_hbm, wq_hbm, bq_hbm, wk_hbm, bk_hbm, wv_hbm, bv_hbm, wo_hbm, keys_hbm, values_hbm, table_hbm, lengths_ref,
    branch_ref, appended_ref,
    x_ref, gain_ref, wq, bq, wk, bk, wv, bv, wo, keys, values, table,
    values_t, mask, bias_rows, scores_ref, weights_ref,
    big, stat, small,
    local_sem, send_sem, recv_sem,
):
    pool, tensor = lax.axis_index("pool"), lax.axis_index("tensor")
    z, y = pool // RING, lax.rem(pool, RING)

    def on_ring(axis, distance):
        if axis == "y":
            return (z * RING + lax.rem(y + distance, RING), tensor)
        if axis == "z":
            return (lax.rem(z + distance, RING) * RING + y, tensor)
        return (pool, lax.rem(tensor + distance, RING))

    partners = {(axis, distance): on_ring(axis, distance) for axis in "yzt" for distance in FAR_FIRST}
    place = {"y": y, "z": z, "t": tensor}
    homes = {"rows": big, "small": small, "stat": stat}

    def slots(step, key):
        kind, at, _, _ = STREAMS[key]
        return homes[kind].at[step, at]

    def fill(step, key, value):
        ref = slots(step, key)
        ref[place[STREAMS[key][2]]] = value.astype(ref.dtype)

    def send(step, *keys):
        for distance in FAR_FIRST:
            for key in keys:
                _, _, ring, at = STREAMS[key]
                own = slots(step, key).at[place[ring]]
                pltpu.make_async_remote_copy(
                    src_ref=own, dst_ref=own,
                    send_sem=send_sem.at[step, at], recv_sem=recv_sem.at[step, at],
                    device_id=partners[ring, distance], device_id_type=MESH,
                ).start()

    def others(step, key, sem):
        part = slots(step, key).at[pl.ds(0, RING - 1)]
        pltpu.make_async_copy(part, part, sem.at[step, STREAMS[key][3]]).wait()

    def receive(step, key):
        others(step, key, recv_sem)
        ref = slots(step, key)
        return [ref[i].astype(F32) for i in range(RING)]

    barrier = pltpu.get_barrier_semaphore()
    for axes in ("yz", "t"):
        for distance, axis in [(distance, axis) for distance in FAR_FIRST for axis in axes]:
            pl.semaphore_signal(barrier, inc=1, device_id=partners[axis, distance], device_id_type=MESH)

    pairs = (
        (x_hbm, x_ref), (gain_hbm, gain_ref), (wq_hbm, wq), (wk_hbm, wk), (wv_hbm, wv), (bq_hbm, bq), (bk_hbm, bk),
        (bv_hbm, bv), (table_hbm, table), (values_hbm, values), (keys_hbm, keys), (wo_hbm, wo),
    )
    loads = [pltpu.make_async_copy(src, dst, local_sem.at[at]) for at, (src, dst) in enumerate(pairs)]
    for load in loads:
        load.start()
    for load in loads[:3]:
        load.wait()

    lane = lax.broadcasted_iota(jnp.int32, (1, LANES), 1)
    lane_seq = lax.rem(lane, SEQS)
    own_seq = lax.broadcasted_iota(jnp.int32, (SEQS, LANES), 0) == lane_seq
    scale = LOG2E / math.sqrt(HEAD)

    def tiled(rows):
        return jnp.concatenate([rows] * GROUP, axis=0)

    def weigh(peaks):
        top = peaks[0]
        for peak in peaks[1:]:
            top = jnp.maximum(top, peak)
        weights = [jnp.exp2(peak - top) for peak in peaks]
        total = weights[0]
        for weight in weights[1:]:
            total = total + weight
        share = 1.0 / total
        return [weight * share for weight in weights], top + jnp.log(total) * LOG2E

    def blend(weights, parts):
        out = weights[0] * parts[0]
        for weight, part in zip(weights[1:], parts[1:]):
            out = out + weight * part
        return out

    def summed(parts):
        total = parts[0]
        for part in parts[1:]:
            total = total + part
        return total

    chains = range(2 * PAIRS)
    pairs_of = [(2 * p, 2 * p + 1) for p in range(PAIRS)]
    span_of = [slice(c * ROWS, (c + 1) * ROWS) for c in chains]

    current = x_ref[...].astype(F32)
    recent = []
    for step in range(STEPS):
        scaled = (current * gain_ref[...].astype(F32)).astype(BF16)
        raw = dot(scaled, wq[...]).astype(BF16)
        for chain in chains:
            own = slots(step, ("A1", chain))
            for at in range(ROWS // SEQS):
                h = chain * (ROWS // SEQS) + at
                own[place[RINGS[chain % 2]], at * SEQS:(at + 1) * SEQS, :] = raw[:, h * HEAD:(h + 1) * HEAD]
        squares = jnp.sum((current * current).T, axis=0, keepdims=True)
        fill(step, ("A1", "squares"), jnp.concatenate([squares, jnp.ones((1, LANES - SEQS), F32)], axis=1))
        if step == 0:
            pl.semaphore_wait(barrier, 3 * (RING - 1))
        for at, pair in enumerate(pairs_of):
            keys_sent = [("A1", chain) for chain in pair]
            send(step, *(keys_sent + [("A1", "squares")] if at == 0 else keys_sent))
        if step == 0:
            for load in loads[3:5]:
                load.wait()
        fill(step, ("A1", "k"), dot(scaled, wk[...]))
        fill(step, ("A1", "v"), dot(scaled, wv[...]))
        send(step, ("A1", "k"), ("A1", "v"))

        if step == 0:
            for load in loads[5:10]:
                load.wait()
            for h in range(GROUP):
                bias_rows[h * SEQS:(h + 1) * SEQS, :] = jnp.broadcast_to(bq[h:h + 1, :].astype(F32), (SEQS, HEAD))
            length_row = jnp.zeros((1, LANES), jnp.int32)
            for s in range(SEQS):
                length_row = jnp.where(lane_seq == s, lengths_ref[s], length_row)
            table_t = tiled(table[...].astype(F32)).T
            blocks = table_t.shape[0]
            left = length_row.astype(F32) - PAGE * lax.broadcasted_iota(jnp.int32, (blocks, LANES), 0).astype(F32)
            token = lax.broadcasted_iota(jnp.int32, (PAGE, LANES), 0).astype(F32)
            first_page = pool * SLOTS
            for slot in range(SLOTS):
                span = pl.ds(slot * PAGE, PAGE)
                wanted = (first_page + slot).astype(F32)
                limit = jnp.max(jnp.where(table_t == wanted, left, 0.0), axis=0, keepdims=True)
                mask[span, :] = jnp.where(token < limit, 0.0, NEG)
                values_t[:HEAD, span] = values[span, :].T
            values_t[HEAD:, :] = jnp.ones((ONES, TOKENS), BF16)

        for at, pair in enumerate(pairs_of):
            for chain in pair:
                fill(step, ("A2", chain), summed(receive(step, ("A1", chain))))
            keys_sent = [("A2", chain) for chain in pair]
            if at == 0:
                fill(step, ("A2", "squares"), summed(receive(step, ("A1", "squares"))))
                keys_sent.append(("A2", "squares"))
            send(step, *keys_sent)
        fill(step, ("A2", "k"), summed(receive(step, ("A1", "k"))))
        fill(step, ("A2", "v"), summed(receive(step, ("A1", "v"))))
        send(step, ("A2", "k"), ("A2", "v"))
        inverse = lax.rsqrt(summed(receive(step, ("A2", "squares"))) / width + EPS)
        inverse = jnp.broadcast_to(inverse, (LANES, LANES)).T[:SEQS]
        raw = jnp.concatenate([summed(receive(step, ("A2", chain))) for chain in chains], axis=0)
        query = (tiled(inverse) * raw + bias_rows[...]).astype(BF16)

        if step == 0:
            loads[10].wait()
        top = jnp.full((8, LANES), NEG, F32)
        for at in range(0, TOKENS, CHUNK):
            span = pl.ds(at, CHUNK)
            scores = dot_rows(keys[span, :], query) * scale + mask[span, :]
            scores_ref[span, :] = scores
            top = jnp.maximum(top, jnp.max(scores.reshape(CHUNK // 8, 8, LANES), axis=0))
        peak = jnp.max(top, axis=0, keepdims=True)
        bound = jnp.maximum(peak, 0.5 * NEG)
        for at in range(0, TOKENS, CHUNK):
            span = pl.ds(at, CHUNK)
            weights_ref[span, :] = jnp.exp2(scores_ref[span, :] - bound).astype(BF16)
        out_t = dot(values_t[...], weights_ref[...])
        total = out_t[HEAD:HEAD + 1]
        some = total > 0.0
        safe = jnp.where(some, total, 1.0)
        log_total = jnp.where(some, peak + jnp.log(safe) * LOG2E, NEG)
        out_t = out_t[:HEAD] * (1.0 / safe)
        for key in (("B1", "first"), ("B1", "second")):
            fill(step, key, log_total)
        for chain in chains:
            fill(step, ("B1", chain), out_t[span_of[chain]])
        for at, pair in enumerate(pairs_of):
            keys_sent = [("B1", chain) for chain in pair]
            send(step, *(keys_sent + [("B1", "first"), ("B1", "second")] if at == 0 else keys_sent))

        latest_key = (inverse * summed(receive(step, ("A2", "k"))) + bk[...].astype(F32)).astype(BF16)
        latest_value = (inverse * summed(receive(step, ("A2", "v"))) + bv[...].astype(F32)).astype(BF16)
        appended_ref[step, 0] = latest_key
        appended_ref[step, 1] = latest_value
        recent.append((latest_key, tiled(latest_value.astype(F32)).T))
        new_scores = [
            jnp.sum(jnp.where(own_seq, dot_rows(key, query), 0.0), axis=0, keepdims=True) * scale for key, _ in recent
        ]
        new_weights, new_total = weigh(new_scores)
        new_out = blend(new_weights, [value for _, value in recent])

        halves = ("first", "second")
        weights = [None, None]
        for at, pair in enumerate(pairs_of):
            for chain in pair:
                which = chain % 2
                if at == 0:
                    weights[which], log_total = weigh(receive(step, ("B1", halves[which])))
                    fill(step, ("B2", halves[which]), log_total)
                fill(step, ("B2", chain), blend(weights[which], receive(step, ("B1", chain))))
            keys_sent = [("B2", chain) for chain in pair]
            send(step, *(keys_sent + [("B2", "first"), ("B2", "second")] if at == 0 else keys_sent))
        for which in range(2):
            weights[which], _ = weigh(receive(step, ("B2", halves[which])) + [new_total])
        attended = [
            blend(weights[chain % 2], receive(step, ("B2", chain)) + [new_out[span_of[chain]]]) for chain in chains
        ]
        attended = jnp.concatenate(attended, axis=0).T.astype(BF16)
        attended = jnp.concatenate([attended[h * SEQS:(h + 1) * SEQS] for h in range(GROUP)], axis=1)
        if step == 0:
            loads[11].wait()
        fill(step, ("C", "layer"), dot(attended, wo[...]))
        send(step, ("C", "layer"))
        layer = summed(receive(step, ("C", "layer")))
        branch_ref[step] = layer.astype(BF16)
        current = (current + layer).astype(BF16).astype(F32)

    for step in range(STEPS):
        for key in STREAMS:
            others(step, key, send_sem)


def shards(
    stream, norm_gain, query_weight, query_bias, key_matrix, key_offset_bias, value_matrix, value_offset_bias,
    out_weight, key_pages, paged_values, block_table, lengths, *, width,
):
    operands = (
        stream, norm_gain.reshape(1, HEAD), query_weight, query_bias.reshape(GROUP, HEAD),
        key_matrix, key_offset_bias.reshape(1, HEAD), value_matrix, value_offset_bias.reshape(1, HEAD),
        out_weight, key_pages.reshape(TOKENS, HEAD), paged_values.reshape(TOKENS, HEAD), block_table, lengths,
    )
    anywhere = pl.BlockSpec(memory_space=pl.ANY)
    branch, appended = pl.pallas_call(
        functools.partial(kernel, width),
        out_shape=(
            jax.ShapeDtypeStruct((STEPS, SEQS, HEAD), BF16),
            jax.ShapeDtypeStruct((STEPS, 2, SEQS, HEAD), BF16),
        ),
        in_specs=[anywhere] * 12 + [pl.BlockSpec(memory_space=pltpu.SMEM)],
        out_specs=(pl.BlockSpec(memory_space=pltpu.VMEM), pl.BlockSpec(memory_space=pltpu.VMEM)),
        scratch_shapes=[pltpu.VMEM(operand.shape, operand.dtype) for operand in operands[:12]] + [
            pltpu.VMEM((HEAD + ONES, TOKENS), BF16),
            pltpu.VMEM((TOKENS, LANES), F32),
            pltpu.VMEM((LANES, HEAD), F32),
            pltpu.VMEM((TOKENS, LANES), F32),
            pltpu.VMEM((TOKENS, LANES), BF16),
            pltpu.VMEM((STEPS, COUNTS["rows"], RING, ROWS, LANES), BF16),
            pltpu.VMEM((STEPS, COUNTS["stat"], RING, 1, LANES), F32),
            pltpu.VMEM((STEPS, COUNTS["small"], RING, SEQS, HEAD), BF16),
            pltpu.SemaphoreType.DMA((12,)),
            pltpu.SemaphoreType.DMA((STEPS, len(STREAMS))),
            pltpu.SemaphoreType.DMA((STEPS, len(STREAMS))),
        ],
        compiler_params=pltpu.CompilerParams(
            collective_id=0, has_side_effects=True, vmem_limit_bytes=64 * 2**20
        ),
        cost_estimate=pl.CostEstimate(flops=400_000_000, bytes_accessed=2_000_000, transcendentals=600_000),
    )(*operands)
    return branch, appended.reshape(STEPS, 2, SEQS, 1, HEAD)


def solution(mesh):
    in_specs = (
        P(None, "pool"), P("pool"), P("pool", "tensor"), P("tensor"), P("pool", "tensor"), P("tensor"),
        P("pool", "tensor"), P("tensor"), P("tensor", "pool"), P("pool", None, "tensor", None),
        P("pool", None, "tensor", None), P(), P(),
    )
    out_specs = (P(None, None, "pool"), P(None, None, None, "tensor", None))
    width = mesh.shape["pool"] * HEAD
    return jax.shard_map(
        functools.partial(shards, width=width), mesh=mesh, in_specs=in_specs, out_specs=out_specs, check_vma=False
    )
```

time: 79 us -> 72.8 us (0.922)
  local copies, waits for them, and re-layouts: 8.1 us -> 1.91 us
    unnamed x28 -> x4, local copies, waits for them, and re-layouts: 8.1 us -> 1.91 us
where the time goes in v2:
time: 72.8 us; the launch traced here: 72.6 us
  Pallas kernels  70 us (96%)
  local copies, waits for them, and re-layouts  1.91 us (3%)
    pallas_call x1, Pallas kernels, shards(): pl.pallas_call(functools.partial(kernel, width), out_shape=(jax.ShapeDtyp...  70 us
    unnamed x4, local copies, waits for them, and re-layouts  1.91 us

profile of v2, /device:TPU:1, one launch (start us, length us, event | category | flops | bytes accessed | tf_op | source)
XLA Modules:
  0.0 72.6 jit_solution(1885565783056717173)
XLA Ops:
  0.6 70.0 %shard_map.140 = (bf16[2,16,128]{2,1,0:T(8,128)(2,1)}, bf16[2,2,16,128]{3,2,1,0:T(8,128)(2,1)}) custom-call(bf16[16,128]{1,0:T(8,128)(2,1)} %x_hbm.1, bf16[1,128]{1,0:T(2,128)(2,1)} %bitcast.13, bf16[128,1024]{1,0:T(8,128)(2,1)} %wq_hbm.1, bf16[8,128]{1,0:T(8,128)(2,1)} %bitcast.12, bf16[128,128]{1,0:T(8,128)(2,1)} %wk_hbm.1, bf16[1,128]{1,0:T(2,128)(2,1)} %bitcast.14, ...), custom_call_target="tpu_custom_call" | custom-call | flops 400000000 | bytes 2000000 | tf_op jit(solution)/shard_map/pallas_call | solution.py:308
  70.6 0.0 copy-start
  70.7 1.3 %copy.18 = bf16[2,16,128]{2,1,0:T(8,128)(2,1)} copy(bf16[2,16,128]{2,1,0:T(8,128)(2,1)} %get-tuple-element.10) | data formatting | bytes 16384
  72.0 0.0 copy-done
  72.0 0.6 copy.19
Async XLA Ops:
  70.6 1.3 %copy-start = (bf16[2,2,16,128]{3,2,1,0:T(8,128)(2,1)S(1)}, bf16[2,2,16,128]{3,2,1,0:T(8,128)(2,1)}, u32[]{:S(2)}) copy-start(bf16[2,2,16,128]{3,2,1,0:T(8,128)(2,1)} %get-tuple-element.5) | copy-start | bytes 49156

commit v3 on v2

--- a/solution.py
+++ b/solution.py
@@ -21,6 +21,7 @@
 LANES = GROUP * SEQS
 TOKENS = SLOTS * PAGE
 ONES = 16
+SHARE = SEQS // RING
 CHUNK = 256
 LOG2E = math.log2(math.e)
 FAR_FIRST = (4, 3, 5, 2, 6, 1, 7)
@@ -38,14 +39,15 @@
     for phase in PHASES:
         for chain in range(2 * PAIRS):
             streams[phase, chain] = ("rows", RINGS[(chain + PHASES.index(phase)) % 2])
-    for phase, name, ring in (("A1", "k", "y"), ("A1", "v", "z"), ("A2", "k", "z"), ("A2", "v", "y"), ("C", "layer", "t")):
-        streams[phase, name] = ("small", ring)
+    streams["C", "layer"] = ("small", "t")
+    for phase, ring in (("A1", "y"), ("A2", "z"), ("B1", "y")):
+        streams[phase, "kv"] = ("kv", ring)
     for phase, name, ring in (
         ("A1", "squares", "y"), ("A2", "squares", "z"),
         ("B1", "first", "y"), ("B1", "second", "z"), ("B2", "first", "z"), ("B2", "second", "y"),
     ):
         streams[phase, name] = ("stat", ring)
-    kinds = {"rows": 0, "small": 0, "stat": 0}
+    kinds = {"rows": 0, "small": 0, "stat": 0, "kv": 0}
     placed = {}
     for at, (key, (kind, ring)) in enumerate(streams.items()):
         placed[key] = (kind, kinds[kind], ring, at)
@@ -66,12 +68,13 @@
 
 def kernel(
     width,
-    x_hbm, gain_hbm, wq_hbm, bq_hbm, wk_hbm, bk_hbm, wv_hbm, bv_hbm, wo_hbm, keys_hbm, values_hbm, table_hbm, lengths_ref,
+    x_hbm, gain_hbm, wq_hbm, bq_hbm, wk_hbm, bk_hbm, wv_hbm, bv_hbm, wo_hbm, keys_hbm, values_hbm, table_hbm, lengths_hbm,
+    branch_hbm, appended_hbm,
+    x_ref, gain_ref, wq, bq, wk, bk, wv, bv, wo, keys, values, table, lengths_ref,
     branch_ref, appended_ref,
-    x_ref, gain_ref, wq, bq, wk, bk, wv, bv, wo, keys, values, table,
     values_t, mask, bias_rows, scores_ref, weights_ref,
-    big, stat, small,
-    local_sem, send_sem, recv_sem,
+    big, stat, small, kv, kv_out,
+    local_sem, out_sem, send_sem, recv_sem,
 ):
     pool, tensor = lax.axis_index("pool"), lax.axis_index("tensor")
     z, y = pool // RING, lax.rem(pool, RING)
@@ -85,7 +88,7 @@
 
     partners = {(axis, distance): on_ring(axis, distance) for axis in "yzt" for distance in FAR_FIRST}
     place = {"y": y, "z": z, "t": tensor}
-    homes = {"rows": big, "small": small, "stat": stat}
+    homes = {"rows": big, "small": small, "stat": stat, "kv": kv}
 
     def slots(step, key):
         kind, at, _, _ = STREAMS[key]
@@ -106,6 +109,17 @@
                     device_id=partners[ring, distance], device_id_type=MESH,
                 ).start()
 
+    def scatter(step, key, pieces):
+        _, _, ring, at = STREAMS[key]
+        ref = slots(step, key)
+        ref[place[ring]] = pieces[place[ring]]
+        for distance in FAR_FIRST:
+            pltpu.make_async_remote_copy(
+                src_ref=pieces.at[lax.rem(place[ring] + distance, RING)], dst_ref=ref.at[place[ring]],
+                send_sem=send_sem.at[step, at], recv_sem=recv_sem.at[step, at],
+                device_id=partners[ring, distance], device_id_type=MESH,
+            ).start()
+
     def others(step, key, sem):
         part = slots(step, key).at[pl.ds(0, RING - 1)]
         pltpu.make_async_copy(part, part, sem.at[step, STREAMS[key][3]]).wait()
@@ -122,7 +136,7 @@
 
     pairs = (
         (x_hbm, x_ref), (gain_hbm, gain_ref), (wq_hbm, wq), (wk_hbm, wk), (wv_hbm, wv), (bq_hbm, bq), (bk_hbm, bk),
-        (bv_hbm, bv), (table_hbm, table), (values_hbm, values), (keys_hbm, keys), (wo_hbm, wo),
+        (bv_hbm, bv), (table_hbm, table), (lengths_hbm, lengths_ref), (values_hbm, values), (keys_hbm, keys), (wo_hbm, wo),
     )
     loads = [pltpu.make_async_copy(src, dst, local_sem.at[at]) for at, (src, dst) in enumerate(pairs)]
     for load in loads:
@@ -164,6 +178,12 @@
     chains = range(2 * PAIRS)
     pairs_of = [(2 * p, 2 * p + 1) for p in range(PAIRS)]
     span_of = [slice(c * ROWS, (c + 1) * ROWS) for c in chains]
+
+    stores = []
+
+    def store(ref, hbm, step, which):
+        stores.append(pltpu.make_async_copy(ref.at[step], hbm.at[step], out_sem.at[step, which]))
+        stores[-1].start()
 
     current = x_ref[...].astype(F32)
     recent = []
@@ -185,12 +205,14 @@
         if step == 0:
             for load in loads[3:5]:
                 load.wait()
-        fill(step, ("A1", "k"), dot(scaled, wk[...]))
-        fill(step, ("A1", "v"), dot(scaled, wv[...]))
-        send(step, ("A1", "k"), ("A1", "v"))
-
-        if step == 0:
-            for load in loads[5:10]:
+        new_key, new_value = dot(scaled, wk[...]), dot(scaled, wv[...])
+        for i in range(RING):
+            kv_out[step, i, :SHARE] = new_key[i * SHARE:(i + 1) * SHARE]
+            kv_out[step, i, SHARE:] = new_value[i * SHARE:(i + 1) * SHARE]
+        scatter(step, ("A1", "kv"), kv_out.at[step])
+
+        if step == 0:
+            for load in loads[5:11]:
                 load.wait()
             for h in range(GROUP):
                 bias_rows[h * SEQS:(h + 1) * SEQS, :] = jnp.broadcast_to(bq[h:h + 1, :].astype(F32), (SEQS, HEAD))
@@ -218,16 +240,15 @@
                 fill(step, ("A2", "squares"), summed(receive(step, ("A1", "squares"))))
                 keys_sent.append(("A2", "squares"))
             send(step, *keys_sent)
-        fill(step, ("A2", "k"), summed(receive(step, ("A1", "k"))))
-        fill(step, ("A2", "v"), summed(receive(step, ("A1", "v"))))
-        send(step, ("A2", "k"), ("A2", "v"))
+        fill(step, ("A2", "kv"), summed(receive(step, ("A1", "kv"))))
+        send(step, ("A2", "kv"))
         inverse = lax.rsqrt(summed(receive(step, ("A2", "squares"))) / width + EPS)
         inverse = jnp.broadcast_to(inverse, (LANES, LANES)).T[:SEQS]
         raw = jnp.concatenate([summed(receive(step, ("A2", chain))) for chain in chains], axis=0)
         query = (tiled(inverse) * raw + bias_rows[...]).astype(BF16)
 
         if step == 0:
-            loads[10].wait()
+            loads[11].wait()
         top = jnp.full((8, LANES), NEG, F32)
         for at in range(0, TOKENS, CHUNK):
             span = pl.ds(at, CHUNK)
@@ -251,18 +272,10 @@
             fill(step, ("B1", chain), out_t[span_of[chain]])
         for at, pair in enumerate(pairs_of):
             keys_sent = [("B1", chain) for chain in pair]
-            send(step, *(keys_sent + [("B1", "first"), ("B1", "second")] if at == 0 else keys_sent))
-
-        latest_key = (inverse * summed(receive(step, ("A2", "k"))) + bk[...].astype(F32)).astype(BF16)
-        latest_value = (inverse * summed(receive(step, ("A2", "v"))) + bv[...].astype(F32)).astype(BF16)
-        appended_ref[step, 0] = latest_key
-        appended_ref[step, 1] = latest_value
-        recent.append((latest_key, tiled(latest_value.astype(F32)).T))
-        new_scores = [
-            jnp.sum(jnp.where(own_seq, dot_rows(key, query), 0.0), axis=0, keepdims=True) * scale for key, _ in recent
-        ]
-        new_weights, new_total = weigh(new_scores)
-        new_out = blend(new_weights, [value for _, value in recent])
+            send(step, *([("B1", "first"), ("B1", "second")] + keys_sent if at == 0 else keys_sent))
+
+        fill(step, ("B1", "kv"), summed(receive(step, ("A2", "kv"))))
+        send(step, ("B1", "kv"))
 
         halves = ("first", "second")
         weights = [None, None]
@@ -274,7 +287,20 @@
                     fill(step, ("B2", halves[which]), log_total)
                 fill(step, ("B2", chain), blend(weights[which], receive(step, ("B1", chain))))
             keys_sent = [("B2", chain) for chain in pair]
-            send(step, *(keys_sent + [("B2", "first"), ("B2", "second")] if at == 0 else keys_sent))
+            send(step, *([("B2", "first"), ("B2", "second")] + keys_sent if at == 0 else keys_sent))
+        parts = receive(step, ("B1", "kv"))
+        latest_key = (inverse * jnp.concatenate([part[:SHARE] for part in parts], axis=0) + bk[...].astype(F32)).astype(BF16)
+        latest_value = (inverse * jnp.concatenate([part[SHARE:] for part in parts], axis=0) + bv[...].astype(F32)).astype(BF16)
+        appended_ref[step, 0] = latest_key
+        appended_ref[step, 1] = latest_value
+        store(appended_ref, appended_hbm, step, 0)
+        recent.append((latest_key, tiled(latest_value.astype(F32)).T))
+        new_scores = [
+            jnp.sum(jnp.where(own_seq, dot_rows(key, query), 0.0), axis=0, keepdims=True) * scale for key, _ in recent
+        ]
+        new_weights, new_total = weigh(new_scores)
+        new_out = blend(new_weights, [value for _, value in recent])
+
         for which in range(2):
             weights[which], _ = weigh(receive(step, ("B2", halves[which])) + [new_total])
         attended = [
@@ -283,13 +309,16 @@
         attended = jnp.concatenate(attended, axis=0).T.astype(BF16)
         attended = jnp.concatenate([attended[h * SEQS:(h + 1) * SEQS] for h in range(GROUP)], axis=1)
         if step == 0:
-            loads[11].wait()
+            loads[12].wait()
         fill(step, ("C", "layer"), dot(attended, wo[...]))
         send(step, ("C", "layer"))
         layer = summed(receive(step, ("C", "layer")))
         branch_ref[step] = layer.astype(BF16)
+        store(branch_ref, branch_hbm, step, 1)
         current = (current + layer).astype(BF16).astype(F32)
 
+    for made in stores:
+        made.wait()
     for step in range(STEPS):
         for key in STREAMS:
             others(step, key, send_sem)
@@ -311,9 +340,12 @@
             jax.ShapeDtypeStruct((STEPS, SEQS, HEAD), BF16),
             jax.ShapeDtypeStruct((STEPS, 2, SEQS, HEAD), BF16),
         ),
-        in_specs=[anywhere] * 12 + [pl.BlockSpec(memory_space=pltpu.SMEM)],
-        out_specs=(pl.BlockSpec(memory_space=pltpu.VMEM), pl.BlockSpec(memory_space=pltpu.VMEM)),
+        in_specs=[anywhere] * 13,
+        out_specs=(anywhere, anywhere),
         scratch_shapes=[pltpu.VMEM(operand.shape, operand.dtype) for operand in operands[:12]] + [
+            pltpu.SMEM((SEQS,), jnp.int32),
+            pltpu.VMEM((STEPS, SEQS, HEAD), BF16),
+            pltpu.VMEM((STEPS, 2, SEQS, HEAD), BF16),
             pltpu.VMEM((HEAD + ONES, TOKENS), BF16),
             pltpu.VMEM((TOKENS, LANES), F32),
             pltpu.VMEM((LANES, HEAD), F32),
@@ -322,7 +354,10 @@
             pltpu.VMEM((STEPS, COUNTS["rows"], RING, ROWS, LANES), BF16),
             pltpu.VMEM((STEPS, COUNTS["stat"], RING, 1, LANES), F32),
             pltpu.VMEM((STEPS, COUNTS["small"], RING, SEQS, HEAD), BF16),
-            pltpu.SemaphoreType.DMA((12,)),
+            pltpu.VMEM((STEPS, COUNTS["kv"], RING, 2 * SHARE, HEAD), F32),
+            pltpu.VMEM((STEPS, RING, 2 * SHARE, HEAD), F32),
+            pltpu.SemaphoreType.DMA((13,)),
+            pltpu.SemaphoreType.DMA((STEPS, 2)),
             pltpu.SemaphoreType.DMA((STEPS, len(STREAMS))),
             pltpu.SemaphoreType.DMA((STEPS, len(STREAMS))),
         ],

time: 72.8 us -> 71.6 us (0.984)
  Pallas kernels: 70 us -> 68.9 us
    pallas_call x1, Pallas kernels: 70 us -> 68.9 us  [shards(): pl.pallas_call(functools.partial(kernel, width), out_shape=(jax.ShapeDtyp...]
where the time goes in v3:
time: 71.6 us; the launch traced here: 71.4 us
  Pallas kernels  68.9 us (96%)
  local copies, waits for them, and re-layouts  1.91 us (3%)
    pallas_call x1, Pallas kernels, shards(): pl.pallas_call(functools.partial(kernel, width), out_shape=(jax.ShapeDtyp...  68.9 us
    unnamed x4, local copies, waits for them, and re-layouts  1.91 us

profile of v3, /device:TPU:1, one launch (start us, length us, event | category | flops | bytes accessed | tf_op | source)
XLA Modules:
  0.0 71.4 jit_solution(9496005383298558444)
XLA Ops:
  0.6 68.9 %shard_map.140 = (bf16[2,16,128]{2,1,0:T(8,128)(2,1)}, bf16[2,2,16,128]{3,2,1,0:T(8,128)(2,1)}) custom-call(bf16[16,128]{1,0:T(8,128)(2,1)} %x_hbm.1, bf16[1,128]{1,0:T(2,128)(2,1)} %bitcast.13, bf16[128,1024]{1,0:T(8,128)(2,1)} %wq_hbm.1, bf16[8,128]{1,0:T(8,128)(2,1)} %bitcast.12, bf16[128,128]{1,0:T(8,128)(2,1)} %wk_hbm.1, bf16[1,128]{1,0:T(2,128)(2,1)} %bitcast.14, ...), custom_call_target="tpu_custom_call" | custom-call | flops 400000000 | bytes 2000000 | tf_op jit(solution)/shard_map/pallas_call | solution.py:337
  69.5 0.0 copy-start
  69.5 1.3 %copy.18 = bf16[2,16,128]{2,1,0:T(8,128)(2,1)} copy(bf16[2,16,128]{2,1,0:T(8,128)(2,1)} %get-tuple-element.10) | data formatting | bytes 16384
  70.8 0.0 copy-done
  70.8 0.6 copy.19
Async XLA Ops:
  69.5 1.3 %copy-start = (bf16[2,2,16,128]{3,2,1,0:T(8,128)(2,1)S(1)}, bf16[2,2,16,128]{3,2,1,0:T(8,128)(2,1)}, u32[]{:S(2)}) copy-start(bf16[2,2,16,128]{3,2,1,0:T(8,128)(2,1)} %get-tuple-element.5) | copy-start | bytes 49156

commit v4 on v3

--- a/solution.py
+++ b/solution.py
@@ -21,10 +21,13 @@
 LANES = GROUP * SEQS
 TOKENS = SLOTS * PAGE
 ONES = 16
+HALF = HEAD // 2
 SHARE = SEQS // RING
 CHUNK = 256
+VMEM_ASKED = 55185 * 1024
 LOG2E = math.log2(math.e)
 FAR_FIRST = (4, 3, 5, 2, 6, 1, 7)
+FAR, NEAR = FAR_FIRST[:3], FAR_FIRST[3:]
 BF16 = jnp.bfloat16
 F32 = jnp.float32
 
@@ -98,8 +101,8 @@
         ref = slots(step, key)
         ref[place[STREAMS[key][2]]] = value.astype(ref.dtype)
 
-    def send(step, *keys):
-        for distance in FAR_FIRST:
+    def send(step, *keys, distances=FAR_FIRST):
+        for distance in distances:
             for key in keys:
                 _, _, ring, at = STREAMS[key]
                 own = slots(step, key).at[place[ring]]
@@ -174,6 +177,11 @@
         for part in parts[1:]:
             total = total + part
         return total
+
+    def send_pairs(step, phase, ahead):
+        for distances in (FAR, NEAR):
+            for at, pair in enumerate(pairs_of):
+                send(step, *((ahead if at == 0 else []) + [(phase, chain) for chain in pair]), distances=distances)
 
     chains = range(2 * PAIRS)
     pairs_of = [(2 * p, 2 * p + 1) for p in range(PAIRS)]
@@ -199,9 +207,7 @@
         fill(step, ("A1", "squares"), jnp.concatenate([squares, jnp.ones((1, LANES - SEQS), F32)], axis=1))
         if step == 0:
             pl.semaphore_wait(barrier, 3 * (RING - 1))
-        for at, pair in enumerate(pairs_of):
-            keys_sent = [("A1", chain) for chain in pair]
-            send(step, *(keys_sent + [("A1", "squares")] if at == 0 else keys_sent))
+        send_pairs(step, "A1", [("A1", "squares")])
         if step == 0:
             for load in loads[3:5]:
                 load.wait()
@@ -229,17 +235,23 @@
                 wanted = (first_page + slot).astype(F32)
                 limit = jnp.max(jnp.where(table_t == wanted, left, 0.0), axis=0, keepdims=True)
                 mask[span, :] = jnp.where(token < limit, 0.0, NEG)
-                values_t[:HEAD, span] = values[span, :].T
-            values_t[HEAD:, :] = jnp.ones((ONES, TOKENS), BF16)
+                page_t = values[span, :].T
+                values_t[:HALF, span] = page_t[:HALF]
+                values_t[HALF + ONES:, span] = page_t[HALF:]
+            values_t[HALF:HALF + ONES, :] = jnp.ones((ONES, TOKENS), BF16)
 
         for at, pair in enumerate(pairs_of):
             for chain in pair:
                 fill(step, ("A2", chain), summed(receive(step, ("A1", chain))))
             keys_sent = [("A2", chain) for chain in pair]
+            distances = FAR_FIRST[:5] if at == 0 else FAR_FIRST[:3]
             if at == 0:
                 fill(step, ("A2", "squares"), summed(receive(step, ("A1", "squares"))))
                 keys_sent.append(("A2", "squares"))
-            send(step, *keys_sent)
+            send(step, *keys_sent, distances=distances)
+            if at == 1:
+                send(step, ("A2", 0), ("A2", 1), ("A2", "squares"), distances=FAR_FIRST[5:])
+                send(step, *keys_sent, distances=FAR_FIRST[3:])
         fill(step, ("A2", "kv"), summed(receive(step, ("A1", "kv"))))
         send(step, ("A2", "kv"))
         inverse = lax.rsqrt(summed(receive(step, ("A2", "squares"))) / width + EPS)
@@ -260,20 +272,24 @@
         for at in range(0, TOKENS, CHUNK):
             span = pl.ds(at, CHUNK)
             weights_ref[span, :] = jnp.exp2(scores_ref[span, :] - bound).astype(BF16)
-        out_t = dot(values_t[...], weights_ref[...])
-        total = out_t[HEAD:HEAD + 1]
+        out_t = dot(values_t[:HALF + ONES, :], weights_ref[...])
+        total = out_t[HALF:HALF + 1]
         some = total > 0.0
         safe = jnp.where(some, total, 1.0)
         log_total = jnp.where(some, peak + jnp.log(safe) * LOG2E, NEG)
-        out_t = out_t[:HEAD] * (1.0 / safe)
-        for key in (("B1", "first"), ("B1", "second")):
+        share = 1.0 / safe
+        ahead = [("B1", "first"), ("B1", "second")]
+        for key in ahead:
             fill(step, key, log_total)
-        for chain in chains:
-            fill(step, ("B1", chain), out_t[span_of[chain]])
-        for at, pair in enumerate(pairs_of):
-            keys_sent = [("B1", chain) for chain in pair]
-            send(step, *([("B1", "first"), ("B1", "second")] + keys_sent if at == 0 else keys_sent))
-
+        for chain in pairs_of[0]:
+            fill(step, ("B1", chain), out_t[span_of[chain]] * share)
+        send(step, *ahead, ("B1", 0), ("B1", 1), distances=FAR)
+        out_t = dot(values_t[HALF + ONES:, :], weights_ref[...])
+        for chain in pairs_of[1]:
+            fill(step, ("B1", chain), out_t[(chain - 2) * ROWS:(chain - 1) * ROWS] * share)
+        send(step, ("B1", 2), ("B1", 3), distances=FAR)
+        send(step, *ahead, ("B1", 0), ("B1", 1), distances=NEAR)
+        send(step, ("B1", 2), ("B1", 3), distances=NEAR)
         fill(step, ("B1", "kv"), summed(receive(step, ("A2", "kv"))))
         send(step, ("B1", "kv"))
 
@@ -287,7 +303,13 @@
                     fill(step, ("B2", halves[which]), log_total)
                 fill(step, ("B2", chain), blend(weights[which], receive(step, ("B1", chain))))
             keys_sent = [("B2", chain) for chain in pair]
-            send(step, *([("B2", "first"), ("B2", "second")] + keys_sent if at == 0 else keys_sent))
+            if at == 0:
+                first_sent = [("B2", "first"), ("B2", "second")] + keys_sent
+                send(step, *first_sent, distances=FAR_FIRST[:5])
+            else:
+                send(step, *keys_sent, distances=FAR)
+                send(step, *first_sent, distances=FAR_FIRST[5:])
+                send(step, *keys_sent, distances=NEAR)
         parts = receive(step, ("B1", "kv"))
         latest_key = (inverse * jnp.concatenate([part[:SHARE] for part in parts], axis=0) + bk[...].astype(F32)).astype(BF16)
         latest_value = (inverse * jnp.concatenate([part[SHARE:] for part in parts], axis=0) + bv[...].astype(F32)).astype(BF16)
@@ -362,7 +384,7 @@
             pltpu.SemaphoreType.DMA((STEPS, len(STREAMS))),
         ],
         compiler_params=pltpu.CompilerParams(
-            collective_id=0, has_side_effects=True, vmem_limit_bytes=64 * 2**20
+            collective_id=0, has_side_effects=True, vmem_limit_bytes=VMEM_ASKED
         ),
         cost_estimate=pl.CostEstimate(flops=400_000_000, bytes_accessed=2_000_000, transcendentals=600_000),
     )(*operands)

time: 71.6 us -> 70.8 us (0.989)
  Pallas kernels: 68.9 us -> 67.9 us
    pallas_call x1, Pallas kernels: 68.9 us -> 67.9 us  [shards(): pl.pallas_call(functools.partial(kernel, width), out_shape=(jax.ShapeDtyp...]
    unnamed x4 -> x16, local copies, waits for them, and re-layouts: 1.91 us -> 2 us
where the time goes in v4:
time: 70.8 us; the launch traced here: 70.6 us
  Pallas kernels  67.9 us (96%)
  local copies, waits for them, and re-layouts  2 us (3%)
    pallas_call x1, Pallas kernels, shards(): pl.pallas_call(functools.partial(kernel, width), out_shape=(jax.ShapeDtyp...  67.9 us
    unnamed x16, local copies, waits for them, and re-layouts  2 us

profile of v4, /device:TPU:1, one launch (start us, length us, event | category | flops | bytes accessed | tf_op | source)
XLA Modules:
  0.0 70.6 jit_solution(8597252350883487793)
XLA Ops:
  0.6 0.0 copy-start.5
  0.6 0.0 copy-start
  0.7 0.0 copy-start.1
  0.7 0.0 copy-start.2
  0.7 0.0 copy-start.3
  0.7 0.0 copy-start.4
  0.7 0.6 copy-done.5
  1.3 0.0 copy-done
  1.3 0.0 copy-done.1
  1.3 0.0 copy-done.2
  1.4 0.0 copy-done.3
  1.4 0.0 copy-done.4
  1.4 67.9 %shard_map.140 = (bf16[2,16,128]{2,1,0:T(8,128)(2,1)S(1)}, bf16[2,2,16,128]{3,2,1,0:T(8,128)(2,1)}) custom-call(bf16[16,128]{1,0:T(8,128)(2,1)S(1)} %copy-done, bf16[1,128]{1,0:T(2,128)(2,1)S(1)} %bitcast.10, bf16[128,1024]{1,0:T(8,128)(2,1)} %wq_hbm.1, bf16[8,128]{1,0:T(8,128)(2,1)S(1)} %bitcast.9, bf16[128,128]{1,0:T(8,128)(2,1)} %wk_hbm.1, ...), custom_call_target="tpu_custom_call" | custom-call | flops 400000000 | bytes 2000000 | tf_op jit(solution)/shard_map/pallas_call | solution.py:359
  69.3 0.0 copy-start.6
  69.3 0.6 copy.18
  69.9 0.1 copy-done.6
  70.0 0.6 copy.19
Async XLA Ops:
  0.6 0.7 copy-start.5
  0.6 0.7 copy-start
  0.7 0.7 copy-start.1
  0.7 0.7 copy-start.2
  0.7 0.7 copy-start.3
  0.7 0.7 copy-start.4
  69.3 0.7 %copy-start.6 = (bf16[2,2,16,128]{3,2,1,0:T(8,128)(2,1)S(1)}, bf16[2,2,16,128]{3,2,1,0:T(8,128)(2,1)}, u32[]{:S(2)}) copy-start(bf16[2,2,16,128]{3,2,1,0:T(8,128)(2,1)} %get-tuple-element.5) | copy-start | bytes 49156

commit v5 on v4

--- a/solution.py
+++ b/solution.py
@@ -21,7 +21,7 @@
 LANES = GROUP * SEQS
 TOKENS = SLOTS * PAGE
 ONES = 16
-HALF = HEAD // 2
+HALF = 32
 SHARE = SEQS // RING
 CHUNK = 256
 VMEM_ASKED = 55185 * 1024
@@ -32,7 +32,8 @@
 F32 = jnp.float32
 
 PAIRS = 2
-ROWS = HEAD // (2 * PAIRS)
+ROWS_OF = (16, 16, 48, 48)
+ROWS = max(ROWS_OF)
 RINGS = "yz"
 PHASES = ("A1", "A2", "B1", "B2")
 
@@ -95,6 +96,8 @@
 
     def slots(step, key):
         kind, at, _, _ = STREAMS[key]
+        if kind == "rows":
+            return homes[kind].at[step, at, :, pl.ds(0, ROWS_OF[key[1]])]
         return homes[kind].at[step, at]
 
     def fill(step, key, value):
@@ -127,6 +130,11 @@
         part = slots(step, key).at[pl.ds(0, RING - 1)]
         pltpu.make_async_copy(part, part, sem.at[step, STREAMS[key][3]]).wait()
 
+    def drain(step, *phases):
+        for key in STREAMS:
+            if key[0] in phases:
+                others(step, key, send_sem)
+
     def receive(step, key):
         others(step, key, recv_sem)
         ref = slots(step, key)
@@ -185,7 +193,7 @@
 
     chains = range(2 * PAIRS)
     pairs_of = [(2 * p, 2 * p + 1) for p in range(PAIRS)]
-    span_of = [slice(c * ROWS, (c + 1) * ROWS) for c in chains]
+    span_of = [slice(sum(ROWS_OF[:c]), sum(ROWS_OF[:c + 1])) for c in chains]
 
     stores = []
 
@@ -200,8 +208,8 @@
         raw = dot(scaled, wq[...]).astype(BF16)
         for chain in chains:
             own = slots(step, ("A1", chain))
-            for at in range(ROWS // SEQS):
-                h = chain * (ROWS // SEQS) + at
+            for at in range(ROWS_OF[chain] // SEQS):
+                h = span_of[chain].start // SEQS + at
                 own[place[RINGS[chain % 2]], at * SEQS:(at + 1) * SEQS, :] = raw[:, h * HEAD:(h + 1) * HEAD]
         squares = jnp.sum((current * current).T, axis=0, keepdims=True)
         fill(step, ("A1", "squares"), jnp.concatenate([squares, jnp.ones((1, LANES - SEQS), F32)], axis=1))
@@ -216,6 +224,8 @@
             kv_out[step, i, :SHARE] = new_key[i * SHARE:(i + 1) * SHARE]
             kv_out[step, i, SHARE:] = new_value[i * SHARE:(i + 1) * SHARE]
         scatter(step, ("A1", "kv"), kv_out.at[step])
+        if step > 0:
+            drain(step - 1, "C")
 
         if step == 0:
             for load in loads[5:11]:
@@ -286,12 +296,13 @@
         send(step, *ahead, ("B1", 0), ("B1", 1), distances=FAR)
         out_t = dot(values_t[HALF + ONES:, :], weights_ref[...])
         for chain in pairs_of[1]:
-            fill(step, ("B1", chain), out_t[(chain - 2) * ROWS:(chain - 1) * ROWS] * share)
+            fill(step, ("B1", chain), out_t[span_of[chain].start - HALF:span_of[chain].stop - HALF] * share)
         send(step, ("B1", 2), ("B1", 3), distances=FAR)
         send(step, *ahead, ("B1", 0), ("B1", 1), distances=NEAR)
         send(step, ("B1", 2), ("B1", 3), distances=NEAR)
         fill(step, ("B1", "kv"), summed(receive(step, ("A2", "kv"))))
         send(step, ("B1", "kv"))
+        drain(step, "A1", "A2")
 
         halves = ("first", "second")
         weights = [None, None]
@@ -310,6 +321,7 @@
                 send(step, *keys_sent, distances=FAR)
                 send(step, *first_sent, distances=FAR_FIRST[5:])
                 send(step, *keys_sent, distances=NEAR)
+        drain(step, "B1")
         parts = receive(step, ("B1", "kv"))
         latest_key = (inverse * jnp.concatenate([part[:SHARE] for part in parts], axis=0) + bk[...].astype(F32)).astype(BF16)
         latest_value = (inverse * jnp.concatenate([part[SHARE:] for part in parts], axis=0) + bv[...].astype(F32)).astype(BF16)
@@ -334,16 +346,18 @@
             loads[12].wait()
         fill(step, ("C", "layer"), dot(attended, wo[...]))
         send(step, ("C", "layer"))
+        drain(step, "B2")
+        if step == STEPS - 1:
+            for made in stores[:2]:
+                made.wait()
         layer = summed(receive(step, ("C", "layer")))
         branch_ref[step] = layer.astype(BF16)
         store(branch_ref, branch_hbm, step, 1)
         current = (current + layer).astype(BF16).astype(F32)
 
-    for made in stores:
+    for made in stores[2:]:
         made.wait()
-    for step in range(STEPS):
-        for key in STREAMS:
-            others(step, key, send_sem)
+    drain(STEPS - 1, "C")
 
 
 def shards(

time: 70.8 us -> 70.6 us (level)
  no operation moved by 1% of the time
where the time goes in v5:
time: 70.6 us; the launch traced here: 70.4 us
  Pallas kernels  67.7 us (96%)
  local copies, waits for them, and re-layouts  2 us (3%)
    pallas_call x1, Pallas kernels, shards(): pl.pallas_call(functools.partial(kernel, width), out_shape=(jax.ShapeDtyp...  67.7 us
    unnamed x16, local copies, waits for them, and re-layouts  2 us

profile of v5, /device:TPU:1, one launch (start us, length us, event | category | flops | bytes accessed | tf_op | source)
XLA Modules:
  0.0 70.4 jit_solution(9783062056590953414)
XLA Ops:
  0.6 0.0 copy-start.5
  0.6 0.0 copy-start
  0.7 0.0 copy-start.1
  0.7 0.0 copy-start.2
  0.7 0.0 copy-start.3
  0.7 0.0 copy-start.4
  0.7 0.6 copy-done.5
  1.3 0.0 copy-done
  1.3 0.0 copy-done.1
  1.3 0.0 copy-done.2
  1.4 0.0 copy-done.3
  1.4 0.0 copy-done.4
  1.4 67.7 %shard_map.140 = (bf16[2,16,128]{2,1,0:T(8,128)(2,1)S(1)}, bf16[2,2,16,128]{3,2,1,0:T(8,128)(2,1)}) custom-call(bf16[16,128]{1,0:T(8,128)(2,1)S(1)} %copy-done, bf16[1,128]{1,0:T(2,128)(2,1)S(1)} %bitcast.10, bf16[128,1024]{1,0:T(8,128)(2,1)} %wq_hbm.1, bf16[8,128]{1,0:T(8,128)(2,1)S(1)} %bitcast.9, bf16[128,128]{1,0:T(8,128)(2,1)} %wk_hbm.1, ...), custom_call_target="tpu_custom_call" | custom-call | flops 400000000 | bytes 2000000 | tf_op jit(solution)/shard_map/pallas_call | solution.py:373
  69.1 0.0 copy-start.6
  69.1 0.6 copy.18
  69.7 0.1 copy-done.6
  69.8 0.6 copy.19
Async XLA Ops:
  0.6 0.7 copy-start.5
  0.6 0.7 copy-start
  0.7 0.7 copy-start.1
  0.7 0.7 copy-start.2
  0.7 0.7 copy-start.3
  0.7 0.7 copy-start.4
  69.1 0.7 %copy-start.6 = (bf16[2,2,16,128]{3,2,1,0:T(8,128)(2,1)S(1)}, bf16[2,2,16,128]{3,2,1,0:T(8,128)(2,1)}, u32[]{:S(2)}) copy-start(bf16[2,2,16,128]{3,2,1,0:T(8,128)(2,1)} %get-tuple-element.5) | copy-start | bytes 49156
